TPU v7x, 32 devices: a whole 2x2x4 slice. The times are simulated.
32 devices in a mesh: groups: 2 (over x), ep: 16 (over z, y, core).
Axes of the slice: x: 2, y: 2, z: 4, core: 2. Of those that a mesh axis runs over, the one named last changes fastest.
Arguments:
- tokens: bfloat16 [2048, 7168], P(('groups', 'ep')), parts along dimension 0, may hold values from -6 to 6
- expert_ids: int32 [2048, 2], P(('groups', 'ep')), parts along dimension 0, may hold values from 0 to 7, all different within a row; in each aligned block of 64 rows (0 to 63, 64 to 127, ...) at most 24 rows name the same one
- gate_scale: float32 [2048, 2], P(('groups', 'ep')), parts along dimension 0, may hold values from 0.2 to 1
- gate_weight: bfloat16 [16, 7168, 512], P('ep'), may hold values from -0.0625 to 0.0625
- up_weight: bfloat16 [16, 7168, 512], P('ep'), may hold values from -0.0625 to 0.0625
- down_weight: bfloat16 [16, 512, 7168], P('ep'), may hold values from -0.1875 to 0.1875
Outputs:
- mixed: bfloat16 [2048, 7168], P(('groups', 'ep')), parts along dimension 0
There are 2 independent parts, one for each index of `groups`. A program takes and returns all parts, laid end to end along the dimension named above; an argument that names none is the same for every part. Nothing has to cross between parts.
Inputs may be any that keep to these rules, and one draw needn't show every extreme that they name: `expert_ids`: each row names 2 different experts. Among the 64 rows of one device no expert is named by more than 24 rows, and in every draw some expert is named by exactly 24 rows of some device.
All inputs are finite; a program needn't handle non-finite values.
Results may differ from a plain program's by a relative error of at most 0.0058.
Values may be sent and summed in bfloat16 or wider, within the bound.
A program may use at most 128 MiB of HBM per device.

v0:
```python
import jax
import jax.numpy as jnp
from jax import lax
from jax.sharding import PartitionSpec as P


def swapped(x, axis, stride):
    return lax.ppermute(x, axis, [(i, i ^ 1 << stride) for i in range(lax.axis_size(axis))])


def expert_partial(block_rows, gate_weight, up_weight, down_weight):
    gate_act = jnp.dot(block_rows, gate_weight[0], preferred_element_type=jnp.float32)
    up_act = jnp.dot(block_rows, up_weight[0], preferred_element_type=jnp.float32)
    hidden = (jax.nn.silu(gate_act) * up_act).astype(jnp.bfloat16)
    return jnp.dot(hidden, down_weight[0], preferred_element_type=jnp.float32)


def shards(tokens, expert_ids, gate_scale, gate_weight, up_weight, down_weight):
    row_count, model_width = tokens.shape
    top_count = expert_ids.shape[1]
    rank_count = lax.axis_size("ep")
    expert_count = rank_count // 2
    capacity = 2 * (3 * row_count * top_count // (4 * expert_count))
    half_cap = capacity // 2
    flat_ids = expert_ids.reshape(-1)
    one_hot = (flat_ids[:, None] == jnp.arange(expert_count, dtype=jnp.int32)[None, :]).astype(
        jnp.int32
    )
    before = jnp.cumsum(one_hot, axis=0) - one_hot
    slot_index = jnp.sum(before * one_hot, axis=1)
    position = flat_ids * capacity + slot_index
    row_index = jnp.arange(row_count * top_count, dtype=jnp.int32) // top_count
    source_row = jnp.zeros((expert_count * capacity,), jnp.int32).at[position].set(row_index)
    filled = (
        jnp.zeros((expert_count * capacity,), jnp.bfloat16)
        .at[position]
        .set(jnp.ones((row_count * top_count,), jnp.bfloat16))
    )
    buffer = tokens[source_row] * filled[:, None]
    received = lax.all_to_all(buffer, "ep", split_axis=0, concat_axis=0, tiled=True)
    partner = swapped(received, "ep", 0)
    stacked = jnp.concatenate([received, partner], axis=0)
    partial_value = expert_partial(stacked, gate_weight, up_weight, down_weight)
    own_count = rank_count * half_cap
    from_partner = swapped(partial_value[own_count:], "ep", 0)
    finished = (partial_value[:own_count] + from_partner).astype(jnp.bfloat16)
    results = lax.all_to_all(finished, "ep", split_axis=0, concat_axis=0, tiled=True)
    picked = results[position].reshape(row_count, top_count, model_width).astype(jnp.float32)
    mixed = jnp.sum(gate_scale[:, :, None] * picked, axis=1)
    return mixed.astype(jnp.bfloat16)


def solution(mesh):
    in_specs = (
        P(("groups", "ep"), None),
        P(("groups", "ep"), None),
        P(("groups", "ep"), None),
        P("ep", None, None),
        P("ep", None, None),
        P("ep", None, None),
    )
    out_specs = P(("groups", "ep"), None)
    return jax.shard_map(shards, mesh=mesh, in_specs=in_specs, out_specs=out_specs, check_vma=False)
```

profile of v0, /device:TPU:13, one launch (start us, length us, event | category | flops | bytes accessed | tf_op | source)
XLA Modules:
  0.0 264.5 jit_solution(12642604082340891739)
XLA Ops:
  0.0 0.0 copy-start
  0.0 0.8 copy.12
  0.9 0.7 broadcast_multiply_fusion.1
  1.5 0.1 eq.15
  1.7 0.1 fusion.8
  1.8 0.2 reduce_window_sum.11
  1.9 0.2 select_reduce_fusion
  2.1 0.1 copy.11
  2.2 0.1 mul.48
  2.4 1.0 scatter_custom_fusion
  3.4 0.0 copy-done
  3.4 3.8 %gather_fusion = bf16[192,7168]{1,0:T(8,128)(2,1)} fusion(bf16[64,7168]{1,0:T(8,128)(2,1)S(1)} %copy-done, s32[1024]{0:T(1024)S(1)} %pad_clamp_fusion.1), kind=kCustom, calls=%fused_computation | custom fusion | bytes 5505792 | tf_op jit(solution)/shard_map/gather | solution.py:39
  7.2 4.4 %gather.9 = bf16[16,12,7168]{2,1,0:T(8,128)(2,1)} reshape(bf16[192,7168]{1,0:T(8,128)(2,1)} %gather_fusion) | data formatting | bytes 5505024 | tf_op jit(solution)/shard_map/gather | solution.py:39
  11.7 1.3 scatter_custom_fusion.1
  13.0 0.1 mul.50
  13.1 2.3 broadcast_multiply_fusion
  15.5 87.5 %all_to_all.21 = bf16[16,12,7168]{2,1,0:T(8,128)(2,1)} all-to-all(bf16[16,12,7168]{2,1,0:T(8,128)(2,1)S(1)} %broadcast_multiply_fusion), channel_id=1, replica_groups=mesh['groups'=2,'ep'=16] {'ep'}, dimensions={0} | all-to-all | bytes 5505024 | tf_op jit(solution)/shard_map/all_to_all | solution.py:40
  102.9 4.5 %all_to_all.15 = bf16[192,7168]{1,0:T(8,128)(2,1)} reshape(bf16[16,12,7168]{2,1,0:T(8,128)(2,1)} %all_to_all.21) | data formatting | bytes 5505024 | tf_op jit(solution)/shard_map/all_to_all | solution.py:40
  107.4 0.2 collective-permute-start
  107.6 2.0 constant_dynamic-update-slice_fusion.1
  109.6 3.1 %collective-permute-done = bf16[192,7168]{1,0:T(8,128)(2,1)S(1)} collective-permute-done((bf16[192,7168]{1,0:T(8,128)(2,1)}, bf16[192,7168]{1,0:T(8,128)(2,1)S(1)}, u32[]{:S(2)}, u32[]{:S(2)}) %collective-permute-start) | collective-permute-done | bytes 2752544 | tf_op jit(solution)/shard_map/ppermute | solution.py:8
  112.7 0.2 constant_dynamic-update-slice_fusion
  112.9 0.0 copy-start.3
  112.9 2.3 copy-done.3
  115.2 5.3 %fusion.2 = f32[384,512]{1,0:T(8,128)S(1)} fusion(bf16[384,7168]{1,0:T(8,128)(2,1)S(1)} %constant_dynamic-update-slice_fusion, bf16[1,7168,512]{2,1,0:T(8,128)(2,1)} %param.10), kind=kOutput, calls=%fused_computation.6 | convolution fusion | flops 2818572288 | bytes 13631488 | tf_op jit(solution)/shard_map/dot_general | solution.py:13
  120.5 16.9 %fusion = f32[384,7168]{1,0:T(8,128)} fusion(bf16[1,512,7168]{2,1,0:T(8,128)(2,1)} %param.11, f32[384,512]{1,0:T(8,128)S(1)} %fusion.2, bf16[384,7168]{1,0:T(8,128)(2,1)} %copy-done.3, bf16[1,7168,512]{2,1,0:T(8,128)(2,1)} %param.9), kind=kOutput, calls=%fused_computation.4 | convolution fusion | flops 5638324224 | bytes 31981568 | tf_op jit(solution)/shard_map/dot_general | solution.py:15
  137.5 0.0 copy-start.2
  137.5 3.2 %slice.13 = f32[192,7168]{1,0:T(8,128)S(1)} slice(f32[384,7168]{1,0:T(8,128)} %fusion), slice={[192:384], [0:7168]} | slice | bytes 11010048 | tf_op jit(solution)/shard_map/slice | solution.py:45
  140.7 0.3 collective-permute-start.1
  141.0 8.8 %collective-permute-done.1 = f32[192,7168]{1,0:T(8,128)S(1)} collective-permute-done((f32[192,7168]{1,0:T(8,128)S(1)}, f32[192,7168]{1,0:T(8,128)S(1)}, u32[]{:S(2)}, u32[]{:S(2)}) %collective-permute-start.1) | collective-permute-done | bytes 5505056 | tf_op jit(solution)/shard_map/ppermute | solution.py:8
  149.8 0.0 copy-done.2
  149.8 2.2 fusion.6
  152.0 0.0 copy-start.4
  152.0 4.5 %all_to_all.16 = bf16[16,12,7168]{2,1,0:T(8,128)(2,1)} reshape(bf16[192,7168]{1,0:T(8,128)(2,1)} %fusion.6) | data formatting | bytes 5505024 | tf_op jit(solution)/shard_map/all_to_all | solution.py:47
  156.5 5.2 %all-to-all-start.1 = ((bf16[16,12,7168]{2,1,0:T(8,128)(2,1)}), bf16[16,12,7168]{2,1,0:T(8,128)(2,1)}, u32[]{:S(2)}, u32[]{:S(2)}) async-start(bf16[16,12,7168]{2,1,0:T(8,128)(2,1)} %all_to_all.16), calls=%async_computation.1 | async-start | bytes 7340032 | tf_op jit(solution)/shard_map/all_to_all | solution.py:47
  161.7 0.0 copy-done.4
  161.7 0.1 copy.10
  161.8 81.1 %all-to-all-done.1 = bf16[16,12,7168]{2,1,0:T(8,128)(2,1)} async-done(((bf16[16,12,7168]{2,1,0:T(8,128)(2,1)}), bf16[16,12,7168]{2,1,0:T(8,128)(2,1)}, u32[]{:S(2)}, u32[]{:S(2)}) %all-to-all-start.1) | async-done | bytes 2752544 | tf_op jit(solution)/shard_map/all_to_all | solution.py:47
  242.9 4.5 %all_to_all.18 = bf16[192,7168]{1,0:T(8,128)(2,1)} reshape(bf16[16,12,7168]{2,1,0:T(8,128)(2,1)} %all-to-all-done.1) | data formatting | bytes 5505024 | tf_op jit(solution)/shard_map/all_to_all | solution.py:47
  247.4 0.0 copy-start.1
  247.4 5.6 %gather_fusion.1 = bf16[128,7168]{1,0:T(8,128)(2,1)S(1)} fusion(bf16[192,7168]{1,0:T(8,128)(2,1)} %all_to_all.18, s32[1024]{0:T(1024)S(1)} %pad_clamp_fusion), kind=kCustom, calls=%fused_computation.1 | custom fusion | bytes 3670528 | tf_op jit(solution)/shard_map/gather | solution.py:48
  253.0 3.5 %reshape.45 = f32[64,2,7168]{2,1,0:T(2,128)} reshape(bf16[128,7168]{1,0:T(8,128)(2,1)S(1)} %gather_fusion.1) | data formatting | bytes 5505024 | tf_op jit(solution)/shard_map/convert_element_type | solution.py:48
  256.5 8.0 %multiply_reduce_fusion = bf16[64,7168]{1,0:T(8,128)(2,1)} fusion(f32[64,2,7168]{2,1,0:T(2,128)} %reshape.45, f32[64,2]{1,0:T(8,128)S(1)} %copy.10), kind=kLoop, calls=%fused_computation.12 | loop fusion | flops 1376256 | bytes 4588032 | tf_op jit(solution)/shard_map/reduce_sum | solution.py:49
  264.5 0.0 copy-done.1
  (6 shorter events, 0.0 us)
Async XLA Ops:
  0.0 3.4 %copy-start = (bf16[64,7168]{1,0:T(8,128)(2,1)S(1)}, bf16[64,7168]{1,0:T(8,128)(2,1)}, u32[]{:S(2)}) copy-start(bf16[64,7168]{1,0:T(8,128)(2,1)} %param.6) | copy-start | bytes 2752516
  107.4 5.3 %collective-permute-start = (bf16[192,7168]{1,0:T(8,128)(2,1)}, bf16[192,7168]{1,0:T(8,128)(2,1)S(1)}, u32[]{:S(2)}, u32[]{:S(2)}) collective-permute-start(bf16[192,7168]{1,0:T(8,128)(2,1)} %all_to_all.15), channel_id=1, source_target_pairs={{0,1},{1,0},{2,3},{3,2},{4,5},{5,4},{6,7},{7,6},{8,9},{9,8},{10,11... | collective-permute-start | bytes 8257544 | tf_op jit(solution)/shard_map/ppermute | solution.py:8
  112.9 2.4 copy-start.3
  137.5 12.3 %copy-start.2 = (f32[384,7168]{1,0:T(8,128)S(1)}, f32[384,7168]{1,0:T(8,128)}, u32[]{:S(2)}) copy-start(f32[384,7168]{1,0:T(8,128)} %fusion) | copy-start | bytes 33030148
  140.7 9.1 %collective-permute-start.1 = (f32[192,7168]{1,0:T(8,128)S(1)}, f32[192,7168]{1,0:T(8,128)S(1)}, u32[]{:S(2)}, u32[]{:S(2)}) collective-permute-start(f32[192,7168]{1,0:T(8,128)S(1)} %slice.13), channel_id=1, source_target_pairs={{0,1},{1,0},{2,3},{3,2},{4,5},{5,4},{6,7},{7,6},{8,9},{9,8},{10,11... | collective-permute-start | bytes 16515080 | tf_op jit(solution)/shard_map/ppermute | solution.py:8
  152.0 9.7 %copy-start.4 = (f32[64,2]{0,1:T(2,128)S(1)}, f32[64,2]{0,1:T(2,128)}, u32[]{:S(2)}) copy-start(f32[64,2]{0,1:T(2,128)} %param.8) | copy-start | bytes 1540
  156.5 86.5 %all-to-all-start.1 = ((bf16[16,12,7168]{2,1,0:T(8,128)(2,1)}), bf16[16,12,7168]{2,1,0:T(8,128)(2,1)}, u32[]{:S(2)}, u32[]{:S(2)}) async-start(bf16[16,12,7168]{2,1,0:T(8,128)(2,1)} %all_to_all.16), calls=%async_computation.1 | async-start | bytes 7340032 | tf_op jit(solution)/shard_map/all_to_all | solution.py:47
  247.4 17.1 %copy-start.1 = (bf16[64,7168]{1,0:T(8,128)(2,1)S(1)}, bf16[64,7168]{1,0:T(8,128)(2,1)}, u32[]{:S(2)}) copy-start(bf16[64,7168]{1,0:T(8,128)(2,1)} %param.6) | copy-start | bytes 2752516
where the time goes:
time: 265 us; the launch traced here: 264 us
  waiting for transfers between devices  93.1 us (35%)
  blocking collectives  87.5 us (33%)
  local copies, waits for them, and re-layouts  42.2 us (16%)
  matrix products  22.2 us (8%)
  other arithmetic  13.7 us (5%)
  starting transfers between devices  5.73 us (2%)
    all_to_all x1, blocking collectives, shards(): lax.all_to_all(buffer, 'ep', split_axis=0, concat_axis=0, tiled=True)  87.5 us
    all_to_all x1, waiting for transfers between devices, shards(): lax.all_to_all(finished, 'ep', split_axis=0, concat_axis=0, tiled=True)  81.1 us
    dot_general x1, matrix products, expert_partial(): return jnp.dot(hidden, down_weight[0], preferred_element_type=jnp.float32)  16.9 us
    ppermute x2, waiting for transfers between devices, swapped(): lax.ppermute(x, axis, [(i, i ^ 1 << stride) for i in range(lax.axis_size(...  12 us
    all_to_all x2, local copies, waits for them, and re-layouts, shards(): lax.all_to_all(finished, 'ep', split_axis=0, concat_axis=0, tiled=True)  8.93 us
    gather x2, local copies, waits for them, and re-layouts, shards(): buffer = tokens[source_row] * filled[:, None]  8.28 us
    reduce_sum x1, other arithmetic, shards(): mixed = jnp.sum(gate_scale[:, :, None] * picked, axis=1)  7.99 us
    gather x1, local copies, waits for them, and re-layouts, shards(): results[position].reshape(row_count, top_count, model_width)  5.58 us
  transfers between devices with their start and end apart: 3, of which 3 were waited for; matrix products, arithmetic and copies ran while one was open for 1% of the time, Pallas kernels for 0%

commit v1 on v0

v1 whole, which is shorter than its diff:
```python
import functools

import jax
import jax.numpy as jnp
from jax import lax
from jax.experimental import pallas as pl
from jax.experimental.pallas import tpu as pltpu
from jax.sharding import PartitionSpec as P

CHUNKS = 8
BF16, F32 = jnp.bfloat16, jnp.float32


def layer_kernel(
    n_ep, cap, ids_ref, ids_t_ref, scale_ref, tok_ref, wg_hbm, wu_hbm, wd_hbm, out_ref,
    send, recv, ret, res, wg, wu, wd, gate_acc, up_acc, hid, mix,
    w_sem, wd_send, wd_recv, send_sem, own_sem, pair_sem, recv_sem, fwd_sem,
    hid_send, hid_recv, ret_sem, res_sem,
):
    me = lax.axis_index("ep")
    chip = me // 2
    core = me % 2
    partner = chip * 2 + 1 - core
    experts = n_ep // 2
    rows, width = tok_ref.shape
    w = width // CHUNKS
    per_core = CHUNKS // 2
    half = width // 2

    def remote(src, dst, ssem, rsem, dev):
        return pltpu.make_async_remote_copy(
            src_ref=src, dst_ref=dst, send_sem=ssem, recv_sem=rsem,
            device_id={"ep": dev}, device_id_type=pl.DeviceIdType.MESH,
        )

    def chip_at(d):
        return lax.rem(chip + d, experts)

    my_cols = pl.ds(pl.multiple_of(core * half, 128), half)
    pair_cols = pl.ds(pl.multiple_of((1 - core) * half, 128), half)
    load_g = pltpu.make_async_copy(wg_hbm.at[0], wg, w_sem.at[0])
    load_u = pltpu.make_async_copy(wu_hbm.at[0], wu, w_sem.at[1])
    load_d = pltpu.make_async_copy(wd_hbm.at[0, :, my_cols], wd.at[core], w_sem.at[2])
    load_g.start()
    load_u.start()
    load_d.start()

    barrier = pltpu.get_barrier_semaphore()
    for i in range(1, n_ep):
        pl.semaphore_signal(
            barrier, inc=1, device_id={"ep": lax.rem(me + i, n_ep)},
            device_id_type=pl.DeviceIdType.MESH,
        )

    shape3 = (experts, cap, rows)
    block = lax.broadcasted_iota(jnp.int32, shape3, 0).reshape(experts * cap, rows)
    slot = lax.broadcasted_iota(jnp.int32, shape3, 1).reshape(experts * cap, rows)
    named = chip + block
    named = jnp.where(named >= experts, named - experts, named)
    hit = (ids_t_ref[0:1, :] == named) | (ids_t_ref[1:2, :] == named)
    r0 = lax.broadcasted_iota(jnp.int32, (rows, rows), 0)
    r1 = lax.broadcasted_iota(jnp.int32, (rows, rows), 1)
    upper = jnp.where(r0 < r1, 1.0, 0.0).astype(BF16)
    lower = jnp.where(r1 < r0, 1.0, 0.0).astype(BF16)
    hit_f = jnp.where(hit, 1.0, 0.0)
    before = jnp.dot(hit_f.astype(BF16), upper, preferred_element_type=F32)
    pick = jnp.where(before == slot.astype(F32), hit_f, 0.0).astype(BF16)

    pl.semaphore_wait(barrier, n_ep - 1)

    def dispatch(k, _):
        cols = pl.ds(pl.multiple_of(k * w, 128), w)
        picked = jnp.dot(pick, tok_ref[:, cols], preferred_element_type=F32)
        send[k] = picked.reshape(experts, cap, w).astype(BF16)
        for d in range(1, experts):
            remote(
                send.at[k, d], recv.at[k, 2 * (experts - d) + core], send_sem.at[k],
                recv_sem.at[k], chip_at(d) * 2 + k % 2,
            ).start()
        remote(
            send.at[k, 0], recv.at[k, core], send_sem.at[k], pair_sem.at[k], partner
        ).start()
        pltpu.make_async_copy(send.at[k, 0], recv.at[k, core], own_sem.at[k]).start()
        return 0

    lax.fori_loop(0, CHUNKS, dispatch, 0)

    give_d = remote(wd_hbm.at[0, :, pair_cols], wd.at[core], wd_send, wd_recv, partner)
    give_d.start()

    column = lax.broadcasted_iota(jnp.int32, (rows, experts * cap), 1)
    block2 = jnp.zeros_like(column)
    for i in range(1, experts):
        block2 = block2 + jnp.where(column >= i * cap, 1, 0)
    slot2 = column - block2 * cap
    named2 = chip + block2
    named2 = jnp.where(named2 >= experts, named2 - experts, named2)
    hit_a = ids_ref[:, 0:1] == named2
    hit_b = ids_ref[:, 1:2] == named2
    hit2 = jnp.where(hit_a | hit_b, 1.0, 0.0)
    before2 = jnp.dot(lower, hit2.astype(BF16), preferred_element_type=F32)
    scale = jnp.where(hit_a, scale_ref[:, 0:1], 0.0) + jnp.where(hit_b, scale_ref[:, 1:2], 0.0)
    scale = jnp.where(before2 == slot2.astype(F32), scale, 0.0)
    high = scale.astype(BF16)
    mix[0:rows] = high
    mix[rows:] = (scale - high.astype(F32)).astype(BF16)

    gate_acc[...] = jnp.zeros_like(gate_acc)
    up_acc[...] = jnp.zeros_like(up_acc)
    load_g.wait()
    load_u.wait()

    def arrived(ref, sem):
        pltpu.make_async_copy(ref, ref, sem).wait()

    def project(k):
        arrived(recv.at[k, core], own_sem.at[k])
        arrived(recv.at[k, 1 - core], pair_sem.at[k])
        x = recv[k].astype(F32).reshape(n_ep * cap, w).astype(BF16)
        depth = pl.ds(pl.multiple_of(k * w, 128), w)
        gate_acc[...] += jnp.dot(x, wg[depth, :], preferred_element_type=F32)
        up_acc[...] += jnp.dot(x, wu[depth, :], preferred_element_type=F32)

    def consume(p, _):
        mine = 2 * p + core
        other = 2 * p + 1 - core
        arrived(recv.at[mine, pl.ds(2, n_ep - 2)], recv_sem.at[mine])
        remote(
            recv.at[mine, pl.ds(2, n_ep - 2)], recv.at[mine, pl.ds(2, n_ep - 2)],
            fwd_sem.at[p], recv_sem.at[mine], partner,
        ).start()
        project(mine)
        arrived(recv.at[other, pl.ds(2, n_ep - 2)], recv_sem.at[other])
        project(other)
        return 0

    lax.fori_loop(0, per_core, consume, 0)

    g = gate_acc[...]
    hid[core] = (g / (1.0 + jnp.exp(-g)) * up_acc[...]).astype(BF16)
    swap = remote(hid.at[core], hid.at[core], hid_send, hid_recv, partner)
    swap.start()
    load_d.wait()
    arrived(wd.at[1 - core], wd_recv)
    arrived(hid.at[1 - core], hid_recv)

    def finish(j, _):
        cols = pl.ds(pl.multiple_of(j * w, 128), w)
        y = jnp.dot(hid[0], wd[0, :, cols], preferred_element_type=F32)
        y += jnp.dot(hid[1], wd[1, :, cols], preferred_element_type=F32)
        ret[j] = y.reshape(n_ep, cap, w).astype(BF16)
        k = core * per_core + j
        for d in range(1, experts):
            for b in range(2):
                remote(
                    ret.at[j, 2 * d + b], res.at[k, experts - d], ret_sem.at[j],
                    res_sem.at[k], chip_at(d) * 2 + b,
                ).start()
        remote(ret.at[j, 1 - core], res.at[k, 0], ret_sem.at[j], res_sem.at[k], partner).start()
        pltpu.make_async_copy(ret.at[j, core], res.at[k, 0], res_sem.at[k]).start()
        return 0

    lax.fori_loop(0, per_core, finish, 0)

    def combine(i, _):
        k = (i % 2) * per_core + i // 2
        arrived(res.at[k], res_sem.at[k])
        y = res[k].astype(F32).reshape(experts * cap, w).astype(BF16)
        both = jnp.dot(mix[...], y, preferred_element_type=F32)
        cols = pl.ds(pl.multiple_of(k * w, 128), w)
        out_ref[:, cols] = (both[0:rows] + both[rows:]).astype(BF16)
        return 0

    lax.fori_loop(0, CHUNKS, combine, 0)

    def drain(k, _):
        arrived(send.at[k], send_sem.at[k])
        return 0

    lax.fori_loop(0, CHUNKS, drain, 0)

    def drain_pairs(j, _):
        mine = 2 * j + core
        arrived(recv.at[mine, pl.ds(2, n_ep - 2)], fwd_sem.at[j])
        arrived(ret.at[j, pl.ds(0, n_ep - 1)], ret_sem.at[j])
        return 0

    lax.fori_loop(0, per_core, drain_pairs, 0)
    swap.wait_send()
    give_d.wait_send()


def shards(tokens, expert_ids, gate_scale, gate_weight, up_weight, down_weight):
    rows, width = tokens.shape
    top = expert_ids.shape[1]
    n_ep = lax.axis_size("ep")
    experts = n_ep // 2
    cap = 2 * (3 * rows * top // (4 * experts))
    cap = -(-cap // 8) * 8
    ff = gate_weight.shape[2]
    w = width // CHUNKS
    per_core = CHUNKS // 2
    vmem = pl.BlockSpec(memory_space=pltpu.VMEM)
    hbm = pl.BlockSpec(memory_space=pl.ANY)
    dma = pltpu.SemaphoreType.DMA
    total = n_ep * cap
    return pl.pallas_call(
        functools.partial(layer_kernel, n_ep, cap),
        out_shape=jax.ShapeDtypeStruct((rows, width), BF16),
        in_specs=[vmem, vmem, vmem, vmem, hbm, hbm, hbm],
        out_specs=vmem,
        scratch_shapes=[
            pltpu.VMEM((CHUNKS, experts, cap, w), BF16),
            pltpu.VMEM((CHUNKS, n_ep, cap, w), BF16),
            pltpu.VMEM((per_core, n_ep, cap, w), BF16),
            pltpu.VMEM((CHUNKS, experts, cap, w), BF16),
            pltpu.VMEM((width, ff), BF16),
            pltpu.VMEM((width, ff), BF16),
            pltpu.VMEM((2, ff, width // 2), BF16),
            pltpu.VMEM((total, ff), F32),
            pltpu.VMEM((total, ff), F32),
            pltpu.VMEM((2, total, ff), BF16),
            pltpu.VMEM((2 * rows, experts * cap), BF16),
            dma((3,)),
            dma,
            dma,
            dma((CHUNKS,)),
            dma((CHUNKS,)),
            dma((CHUNKS,)),
            dma((CHUNKS,)),
            dma((per_core,)),
            dma,
            dma,
            dma((per_core,)),
            dma((CHUNKS,)),
        ],
        compiler_params=pltpu.CompilerParams(
            collective_id=0, has_side_effects=True, vmem_limit_bytes=60 * 1024 * 1024
        ),
        cost_estimate=pl.CostEstimate(
            flops=6 * total * width * ff, bytes_accessed=6 * width * ff,
            transcendentals=total * ff,
        ),
    )(expert_ids, expert_ids.T, gate_scale, tokens, gate_weight, up_weight, down_weight)


def solution(mesh):
    in_specs = (
        P(("groups", "ep"), None),
        P(("groups", "ep"), None),
        P(("groups", "ep"), None),
        P("ep", None, None),
        P("ep", None, None),
        P("ep", None, None),
    )
    out_specs = P(("groups", "ep"), None)
    return jax.shard_map(shards, mesh=mesh, in_specs=in_specs, out_specs=out_specs, check_vma=False)
```

time: 265 us -> 138 us (0.52)
  Pallas kernels: 0 us -> 133 us
  waiting for transfers between devices: 93.1 us -> 0 us
  blocking collectives: 87.5 us -> 0 us
  local copies, waits for them, and re-layouts: 42.2 us -> 4.91 us
  matrix products: 22.2 us -> 0 us
  other arithmetic: 13.7 us -> 0 us
  starting transfers between devices: 5.73 us -> 0 us
    pallas_call x0 -> x1, Pallas kernels: none -> 133 us  [shards(): pl.pallas_call(functools.partial(layer_kernel, n_ep, cap), out_shape=jax....]
    all_to_all x1 -> x0, blocking collectives: 87.5 us -> none  [shards(): lax.all_to_all(buffer, 'ep', split_axis=0, concat_axis=0, tiled=True)]
    all_to_all x1 -> x0, waiting for transfers between devices: 81.1 us -> none  [shards(): lax.all_to_all(finished, 'ep', split_axis=0, concat_axis=0, tiled=True)]
    dot_general x2 -> x0, matrix products: 22.2 us -> none  [the longest x1 16.9 us: expert_partial(): return jnp.dot(hidden, down_weight[0], preferred_element_type=jnp.float32)]
    gather x3 -> x0, local copies, waits for them, and re-layouts: 13.9 us -> none  [the longest x2 8.28 us: shards(): buffer = tokens[source_row] * filled[:, None]]
    all_to_all x3 -> x0, local copies, waits for them, and re-layouts: 13.4 us -> none  [the longest x2 8.93 us: shards(): lax.all_to_all(finished, 'ep', split_axis=0, concat_axis=0, tiled=True)]
    ppermute x2 -> x0, waiting for transfers between devices: 12 us -> none  [swapped(): lax.ppermute(x, axis, [(i, i ^ 1 << stride) for i in range(lax.axis_size(...]
    reduce_sum x2 -> x0, other arithmetic: 8.16 us -> none  [the longest x1 7.99 us: shards(): mixed = jnp.sum(gate_scale[:, :, None] * picked, axis=1)]
  transfers between devices with their start and end apart: 3 -> 0, of which waited for: 3 -> 0; matrix products, arithmetic and copies ran while one was open for 1% -> 0% of each run, Pallas kernels for 0% -> 0%
where the time goes in v1:
time: 138 us
  Pallas kernels  133 us (96%)
  local copies, waits for them, and re-layouts  4.91 us (4%)
    pallas_call x1, Pallas kernels, shards(): pl.pallas_call(functools.partial(layer_kernel, n_ep, cap), out_shape=jax....  133 us
    unnamed x3, local copies, waits for them, and re-layouts  4.91 us

profile of v1, /device:TPU:13, one launch (start us, length us, event | category | flops | bytes accessed | tf_op | source)
XLA Modules:
  0.0 137.7 jit_solution(55884661547062542)
XLA Ops:
  0.0 1.4 copy.8.scale_ref
  1.4 1.4 %copy.7.ids_ref = s32[64,2]{1,0:T(8,128)} copy(s32[64,2]{0,1:T(2,128)} %param.7) | data formatting | bytes 1024 | tf_op args[1]
  2.8 132.7 %shard_map.64 = bf16[64,7168]{1,0:T(8,128)(2,1)} custom-call(s32[64,2]{1,0:T(8,128)} %copy.7.ids_ref, s32[2,64]{1,0:T(2,128)} %bitcast.1, f32[64,2]{1,0:T(8,128)} %copy.8.scale_ref, bf16[64,7168]{1,0:T(8,128)(2,1)} %tok_ref.1, bf16[1,7168,512]{2,1,0:T(8,128)(2,1)} %wg_hbm.1, bf16[1,7168,512]{2,1,0:T(8,128)(2,1)} %wu_hbm.1, bf16[1,512,7168]{2,1,0:T(8,128)(2,1)} %wd_hbm.1), custom_call_target="tpu_custom_call" | custom-call | flops 8455716864 | bytes 22020096 | tf_op jit(solution)/shard_map/pallas_call | solution.py:207
  135.5 2.2 %copy.10 = bf16[64,7168]{1,0:T(8,128)(2,1)} copy(bf16[64,7168]{1,0:T(8,128)(2,1)} %shard_map.64) | data formatting | bytes 1835008

commit v2 on v1

v2 whole, which is shorter than its diff:
```python
import functools

import jax
import jax.numpy as jnp
from jax import lax
from jax.experimental import pallas as pl
from jax.experimental.pallas import tpu as pltpu
from jax.sharding import PartitionSpec as P

CHUNKS = 8
BF16, F32 = jnp.bfloat16, jnp.float32


def layer_kernel(
    n_ep, cap, ids_ref, scale_ref, tok_ref, wg_hbm, wu_hbm, wd_hbm, out_ref,
    send, recv, ret, res, raw, far_out, far_in, near, far_ids, far_scale,
    wg, wu, wd, gate_acc, up_acc, hid, picks, mixes,
    w_sem, wd_sem, meta_sem, raw_send, raw_recv, send_sem, own_sem, pair_sem, recv_sem,
    fwd_sem, hid_sem, ret_sem, res_sem, far_send, far_recv,
):
    me = lax.axis_index("ep")
    core = me % 2
    place = (me // 2) % (n_ep // 4)
    side = me // (n_ep // 2)
    span = n_ep // 4
    first = side * (n_ep // 2)
    partner = first + place * 2 + 1 - core
    twin = (1 - side) * (n_ep // 2) + place * 2 + core
    rows, width = tok_ref.shape
    w = width // CHUNKS
    per_core = CHUNKS // 2
    half = width // 2
    slots = span * cap

    def remote(src, dst, ssem, rsem, dev):
        return pltpu.make_async_remote_copy(
            src_ref=src, dst_ref=dst, send_sem=ssem, recv_sem=rsem,
            device_id={"ep": dev}, device_id_type=pl.DeviceIdType.MESH,
        )

    def near_device(d, b):
        return first + lax.rem(place + d, span) * 2 + b

    def columns(k):
        return pl.ds(pl.multiple_of(k * w, 128), w)

    def arrived(ref, sem):
        pltpu.make_async_copy(ref, ref, sem).wait()

    my_cols = pl.ds(pl.multiple_of(core * half, 128), half)
    pair_cols = pl.ds(pl.multiple_of((1 - core) * half, 128), half)
    load_g = pltpu.make_async_copy(wg_hbm.at[0], wg, w_sem.at[0])
    load_u = pltpu.make_async_copy(wu_hbm.at[0], wu, w_sem.at[1])
    load_d = pltpu.make_async_copy(wd_hbm.at[0, :, my_cols], wd.at[core], w_sem.at[2])
    load_g.start()
    load_u.start()
    load_d.start()

    barrier = pltpu.get_barrier_semaphore()
    for i in range(1, n_ep // 2):
        pl.semaphore_signal(
            barrier, inc=1, device_id={"ep": first + lax.rem(me + i, n_ep // 2)},
            device_id_type=pl.DeviceIdType.MESH,
        )
    pl.semaphore_signal(
        barrier, inc=1, device_id={"ep": twin}, device_id_type=pl.DeviceIdType.MESH
    )

    shape3 = (span, cap, rows)
    block = lax.broadcasted_iota(jnp.int32, shape3, 0).reshape(slots, rows)
    slot = lax.broadcasted_iota(jnp.int32, shape3, 1).reshape(slots, rows).astype(F32)
    named = place + block
    named = jnp.where(named >= span, named - span, named) + side * span
    r0 = lax.broadcasted_iota(jnp.int32, (rows, rows), 0)
    r1 = lax.broadcasted_iota(jnp.int32, (rows, rows), 1)
    earlier = jnp.where(r0 < r1, 1.0, 0.0).astype(BF16)
    unit = jnp.where(r0 == r1, 1.0, 0.0).astype(BF16)

    def plan(which, ids, scales):
        hit_a = ids[0:1, :] == named
        hit_b = ids[1:2, :] == named
        hit = jnp.where(hit_a | hit_b, 1.0, 0.0)
        before = jnp.dot(hit.astype(BF16), earlier, preferred_element_type=F32)
        hit = jnp.where(before == slot, hit, 0.0)
        picks[which] = hit.astype(BF16)
        scale = hit * jnp.where(hit_a, scales[0:1, :], scales[1:2, :])
        high = scale.astype(BF16)
        low = (scale - high.astype(F32)).astype(BF16)
        for i, term in enumerate((high, low)):
            mixes[which, i * rows:(i + 1) * rows] = lax.dot_general(
                unit, term, (((1,), (1,)), ((), ())), preferred_element_type=F32
            ).astype(BF16)

    pl.semaphore_wait(barrier, n_ep // 2)

    give_ids = remote(ids_ref, far_ids, meta_sem.at[0], meta_sem.at[1], twin)
    give_scale = remote(scale_ref, far_scale, meta_sem.at[2], meta_sem.at[3], twin)
    give_ids.start()
    give_scale.start()

    def cross(k, _):
        remote(tok_ref.at[:, columns(k)], raw.at[k], raw_send.at[k], raw_recv.at[k], twin).start()
        return 0

    lax.fori_loop(0, CHUNKS, cross, 0)
    plan(0, ids_ref, scale_ref)

    def spread(k, kind, x):
        picked = jnp.dot(picks[kind], x, preferred_element_type=F32)
        send[k, kind] = picked.reshape(span, cap, w).astype(BF16)
        for d in range(1, span):
            remote(
                send.at[k, kind, d], recv.at[k, 4 * (span - d) + 2 * core + kind],
                send_sem.at[k], recv_sem.at[k], near_device(d, k % 2),
            ).start()
        mine = recv.at[k, 2 * core + kind]
        remote(send.at[k, kind, 0], mine, send_sem.at[k], pair_sem.at[k], partner).start()
        pltpu.make_async_copy(send.at[k, kind, 0], mine, own_sem.at[k]).start()

    def relay(k):
        spread(k, 0, tok_ref[:, columns(k)])
        arrived(raw.at[k], raw_recv.at[k])
        spread(k, 1, raw[k])

    def project(k):
        arrived(recv.at[k, pl.ds(2 * core, 2)], own_sem.at[k])
        arrived(recv.at[k, pl.ds(2 - 2 * core, 2)], pair_sem.at[k])
        x = recv[k].astype(F32).reshape(n_ep * cap, w).astype(BF16)
        depth = columns(k)
        gate_acc[...] += jnp.dot(x, wg[depth, :], preferred_element_type=F32)
        up_acc[...] += jnp.dot(x, wu[depth, :], preferred_element_type=F32)

    def consume(p):
        mine = 2 * p + core
        other = 2 * p + 1 - core
        direct = recv.at[mine, pl.ds(4, n_ep - 4)]
        arrived(direct, recv_sem.at[mine])
        remote(direct, direct, fwd_sem.at[p], recv_sem.at[mine], partner).start()
        project(mine)
        arrived(recv.at[other, pl.ds(4, n_ep - 4)], recv_sem.at[other])
        project(other)

    gate_acc[...] = jnp.zeros_like(gate_acc)
    up_acc[...] = jnp.zeros_like(up_acc)
    give_ids.wait_recv()
    give_scale.wait_recv()
    plan(1, far_ids, far_scale)
    relay(0)
    relay(1)
    give_d = remote(wd_hbm.at[0, :, pair_cols], wd.at[core], wd_sem.at[0], wd_sem.at[1], partner)
    give_d.start()
    load_g.wait()
    load_u.wait()

    def step(p, _):
        relay(2 * p)
        relay(2 * p + 1)
        consume(p - 1)
        return 0

    lax.fori_loop(1, per_core, step, 0)
    consume(per_core - 1)

    g = gate_acc[...]
    hid[core] = (g / (1.0 + jnp.exp(-g)) * up_acc[...]).astype(BF16)
    swap = remote(hid.at[core], hid.at[core], hid_sem.at[0], hid_sem.at[1], partner)
    swap.start()
    load_d.wait()
    arrived(wd.at[1 - core], wd_sem.at[1])
    arrived(hid.at[1 - core], hid_sem.at[1])

    def finish(j, _):
        cols = columns(j)
        y = jnp.dot(hid[0], wd[0, :, cols], preferred_element_type=F32)
        y += jnp.dot(hid[1], wd[1, :, cols], preferred_element_type=F32)
        ret[j] = y.reshape(n_ep, cap, w).astype(BF16)
        k = core * per_core + j
        for d in range(1, span):
            for b in range(2):
                remote(
                    ret.at[j, pl.ds(4 * d + 2 * b, 2)], res.at[k, span - d], ret_sem.at[j],
                    res_sem.at[k], near_device(d, b),
                ).start()
        remote(
            ret.at[j, pl.ds(2 - 2 * core, 2)], res.at[k, 0], ret_sem.at[j], res_sem.at[k], partner
        ).start()
        pltpu.make_async_copy(
            ret.at[j, pl.ds(2 * core, 2)], res.at[k, 0], res_sem.at[k]
        ).start()
        return 0

    lax.fori_loop(0, per_core, finish, 0)

    def chunk(i):
        return (i % 2) * per_core + i // 2

    def mixed(k, kind):
        y = res[k, :, kind].astype(F32).reshape(slots, w).astype(BF16)
        both = jnp.dot(mixes[kind], y, preferred_element_type=F32)
        return both[0:rows] + both[rows:]

    def gather(i, _):
        k = chunk(i)
        arrived(res.at[k], res_sem.at[k])
        far_out[k] = mixed(k, 1).astype(BF16)
        remote(far_out.at[k], far_in.at[k], far_send.at[k], far_recv.at[k], twin).start()
        near[k] = mixed(k, 0)
        return 0

    lax.fori_loop(0, CHUNKS, gather, 0)

    def combine(i, _):
        k = chunk(i)
        arrived(far_in.at[k], far_recv.at[k])
        out_ref[:, columns(k)] = (near[k] + far_in[k].astype(F32)).astype(BF16)
        arrived(raw.at[k], raw_send.at[k])
        arrived(send.at[k], send_sem.at[k])
        arrived(far_out.at[k], far_send.at[k])
        return 0

    lax.fori_loop(0, CHUNKS, combine, 0)

    def drain_pairs(j, _):
        mine = 2 * j + core
        arrived(recv.at[mine, pl.ds(4, n_ep - 4)], fwd_sem.at[j])
        arrived(ret.at[j, pl.ds(0, n_ep - 2)], ret_sem.at[j])
        return 0

    lax.fori_loop(0, per_core, drain_pairs, 0)
    swap.wait_send()
    give_d.wait_send()
    give_ids.wait_send()
    give_scale.wait_send()


def shards(tokens, expert_ids, gate_scale, gate_weight, up_weight, down_weight):
    rows, width = tokens.shape
    top = expert_ids.shape[1]
    n_ep = lax.axis_size("ep")
    experts = n_ep // 2
    span = experts // 2
    cap = 2 * (3 * rows * top // (4 * experts))
    cap = -(-cap // 8) * 8
    ff = gate_weight.shape[2]
    w = width // CHUNKS
    per_core = CHUNKS // 2
    vmem = pl.BlockSpec(memory_space=pltpu.VMEM)
    hbm = pl.BlockSpec(memory_space=pl.ANY)
    dma = pltpu.SemaphoreType.DMA
    total = n_ep * cap
    return pl.pallas_call(
        functools.partial(layer_kernel, n_ep, cap),
        out_shape=jax.ShapeDtypeStruct((rows, width), BF16),
        in_specs=[vmem, vmem, vmem, hbm, hbm, hbm],
        out_specs=vmem,
        scratch_shapes=[
            pltpu.VMEM((CHUNKS, 2, span, cap, w), BF16),
            pltpu.VMEM((CHUNKS, n_ep, cap, w), BF16),
            pltpu.VMEM((per_core, n_ep, cap, w), BF16),
            pltpu.VMEM((CHUNKS, span, 2, cap, w), BF16),
            pltpu.VMEM((CHUNKS, rows, w), BF16),
            pltpu.VMEM((CHUNKS, rows, w), BF16),
            pltpu.VMEM((CHUNKS, rows, w), BF16),
            pltpu.VMEM((CHUNKS, rows, w), F32),
            pltpu.VMEM((top, rows), jnp.int32),
            pltpu.VMEM((top, rows), F32),
            pltpu.VMEM((width, ff), BF16),
            pltpu.VMEM((width, ff), BF16),
            pltpu.VMEM((2, ff, width // 2), BF16),
            pltpu.VMEM((total, ff), F32),
            pltpu.VMEM((total, ff), F32),
            pltpu.VMEM((2, total, ff), BF16),
            pltpu.VMEM((2, span * cap, rows), BF16),
            pltpu.VMEM((2, 2 * rows, span * cap), BF16),
            dma((3,)),
            dma((2,)),
            dma((4,)),
            dma((CHUNKS,)),
            dma((CHUNKS,)),
            dma((CHUNKS,)),
            dma((CHUNKS,)),
            dma((CHUNKS,)),
            dma((CHUNKS,)),
            dma((per_core,)),
            dma((2,)),
            dma((per_core,)),
            dma((CHUNKS,)),
            dma((CHUNKS,)),
            dma((CHUNKS,)),
        ],
        compiler_params=pltpu.CompilerParams(
            collective_id=0, has_side_effects=True, vmem_limit_bytes=60 * 1024 * 1024
        ),
        cost_estimate=pl.CostEstimate(
            flops=6 * total * width * ff, bytes_accessed=6 * width * ff,
            transcendentals=total * ff,
        ),
    )(expert_ids.T, gate_scale.T, tokens, gate_weight, up_weight, down_weight)


def solution(mesh):
    in_specs = (
        P(("groups", "ep"), None),
        P(("groups", "ep"), None),
        P(("groups", "ep"), None),
        P("ep", None, None),
        P("ep", None, None),
        P("ep", None, None),
    )
    out_specs = P(("groups", "ep"), None)
    return jax.shard_map(shards, mesh=mesh, in_specs=in_specs, out_specs=out_specs, check_vma=False)
```

time: 138 us -> 126 us (0.913)
  Pallas kernels: 133 us -> 122 us
  local copies, waits for them, and re-layouts: 4.91 us -> 2.16 us
    pallas_call x1, Pallas kernels: 133 us -> 122 us  [shards(): pl.pallas_call(functools.partial(layer_kernel, n_ep, cap), out_shape=jax....]
    unnamed x3 -> x1, local copies, waits for them, and re-layouts: 4.91 us -> 2.16 us
where the time goes in v2:
time: 126 us; the launch traced here: 125 us
  Pallas kernels  122 us (97%)
  local copies, waits for them, and re-layouts  2.16 us (2%)
    pallas_call x1, Pallas kernels, shards(): pl.pallas_call(functools.partial(layer_kernel, n_ep, cap), out_shape=jax....  122 us

profile of v2, /device:TPU:13, one launch (start us, length us, event | category | flops | bytes accessed | tf_op | source)
XLA Modules:
  0.0 124.7 jit_solution(16033822652587196958)
XLA Ops:
  0.0 122.5 %shard_map.64 = bf16[64,7168]{1,0:T(8,128)(2,1)} custom-call(s32[2,64]{1,0:T(2,128)} %bitcast.2, f32[2,64]{1,0:T(2,128)} %bitcast.3, bf16[64,7168]{1,0:T(8,128)(2,1)} %tok_ref.1, bf16[1,7168,512]{2,1,0:T(8,128)(2,1)} %wg_hbm.1, bf16[1,7168,512]{2,1,0:T(8,128)(2,1)} %wu_hbm.1, bf16[1,512,7168]{2,1,0:T(8,128)(2,1)} %wd_hbm.1), custom_call_target="tpu_custom_call" | custom-call | flops 8455716864 | bytes 22020096 | tf_op jit(solution)/shard_map/pallas_call | solution.py:251
  122.5 2.2 %copy.8 = bf16[64,7168]{1,0:T(8,128)(2,1)} copy(bf16[64,7168]{1,0:T(8,128)(2,1)} %shard_map.64) | data formatting | bytes 1835008

commit v3 on v2

--- a/solution.py
+++ b/solution.py
@@ -7,7 +7,7 @@
 from jax.experimental.pallas import tpu as pltpu
 from jax.sharding import PartitionSpec as P
 
-CHUNKS = 8
+CHUNKS = 14
 BF16, F32 = jnp.bfloat16, jnp.float32
 
 

time: 126 us -> 130 us (1.032)
  Pallas kernels: 122 us -> 126 us
    pallas_call x1, Pallas kernels: 122 us -> 126 us  [shards(): pl.pallas_call(functools.partial(layer_kernel, n_ep, cap), out_shape=jax....]
where the time goes in v3:
time: 130 us; the launch traced here: 129 us
  Pallas kernels  126 us (97%)
  local copies, waits for them, and re-layouts  2.16 us (2%)
    pallas_call x1, Pallas kernels, shards(): pl.pallas_call(functools.partial(layer_kernel, n_ep, cap), out_shape=jax....  126 us

profile of v3, /device:TPU:13, one launch (start us, length us, event | category | flops | bytes accessed | tf_op | source)
XLA Modules:
  0.0 128.5 jit_solution(13280855039540918702)
XLA Ops:
  0.0 126.3 %shard_map.64 = bf16[64,7168]{1,0:T(8,128)(2,1)} custom-call(s32[2,64]{1,0:T(2,128)} %bitcast.2, f32[2,64]{1,0:T(2,128)} %bitcast.3, bf16[64,7168]{1,0:T(8,128)(2,1)} %tok_ref.1, bf16[1,7168,512]{2,1,0:T(8,128)(2,1)} %wg_hbm.1, bf16[1,7168,512]{2,1,0:T(8,128)(2,1)} %wu_hbm.1, bf16[1,512,7168]{2,1,0:T(8,128)(2,1)} %wd_hbm.1), custom_call_target="tpu_custom_call" | custom-call | flops 8455716864 | bytes 22020096 | tf_op jit(solution)/shard_map/pallas_call | solution.py:251
  126.3 2.2 %copy.8 = bf16[64,7168]{1,0:T(8,128)(2,1)} copy(bf16[64,7168]{1,0:T(8,128)(2,1)} %shard_map.64) | data formatting | bytes 1835008

commit v4 on v2

--- a/solution.py
+++ b/solution.py
@@ -25,7 +25,7 @@
     span = n_ep // 4
     first = side * (n_ep // 2)
     partner = first + place * 2 + 1 - core
-    twin = (1 - side) * (n_ep // 2) + place * 2 + core
+    twin = (1 - side) * (n_ep // 2) + lax.rem(place + span // 2, span) * 2 + core
     rows, width = tok_ref.shape
     w = width // CHUNKS
     per_core = CHUNKS // 2
@@ -118,7 +118,12 @@
         pltpu.make_async_copy(send.at[k, kind, 0], mine, own_sem.at[k]).start()
 
     def relay(k):
-        spread(k, 0, tok_ref[:, columns(k)])
+        nxt = k + 2
+
+        @pl.when(nxt < CHUNKS)
+        def _():
+            spread(nxt, 0, tok_ref[:, columns(nxt)])
+
         arrived(raw.at[k], raw_recv.at[k])
         spread(k, 1, raw[k])
 
@@ -142,6 +147,8 @@
 
     gate_acc[...] = jnp.zeros_like(gate_acc)
     up_acc[...] = jnp.zeros_like(up_acc)
+    spread(0, 0, tok_ref[:, columns(0)])
+    spread(1, 0, tok_ref[:, columns(1)])
     give_ids.wait_recv()
     give_scale.wait_recv()
     plan(1, far_ids, far_scale)
@@ -155,10 +162,13 @@
     def step(p, _):
         relay(2 * p)
         relay(2 * p + 1)
-        consume(p - 1)
-        return 0
-
-    lax.fori_loop(1, per_core, step, 0)
+        consume(p - 2)
+        return 0
+
+    relay(2)
+    relay(3)
+    lax.fori_loop(2, per_core, step, 0)
+    consume(per_core - 2)
     consume(per_core - 1)
 
     g = gate_acc[...]

time: 126 us -> 121 us (0.960)
  Pallas kernels: 122 us -> 119 us
    pallas_call x1, Pallas kernels: 122 us -> 119 us  [shards(): pl.pallas_call(functools.partial(layer_kernel, n_ep, cap), out_shape=jax....]
where the time goes in v4:
time: 121 us
  Pallas kernels  119 us (98%)
  local copies, waits for them, and re-layouts  2.16 us (2%)
    pallas_call x1, Pallas kernels, shards(): pl.pallas_call(functools.partial(layer_kernel, n_ep, cap), out_shape=jax....  119 us

profile of v4, /device:TPU:13, one launch (start us, length us, event | category | flops | bytes accessed | tf_op | source)
XLA Modules:
  0.0 120.9 jit_solution(8987165607634242416)
XLA Ops:
  0.0 118.7 %shard_map.64 = bf16[64,7168]{1,0:T(8,128)(2,1)} custom-call(s32[2,64]{1,0:T(2,128)} %bitcast.2, f32[2,64]{1,0:T(2,128)} %bitcast.3, bf16[64,7168]{1,0:T(8,128)(2,1)} %tok_ref.1, bf16[1,7168,512]{2,1,0:T(8,128)(2,1)} %wg_hbm.1, bf16[1,7168,512]{2,1,0:T(8,128)(2,1)} %wu_hbm.1, bf16[1,512,7168]{2,1,0:T(8,128)(2,1)} %wd_hbm.1), custom_call_target="tpu_custom_call" | custom-call | flops 8455716864 | bytes 22020096 | tf_op jit(solution)/shard_map/pallas_call | solution.py:261
  118.7 2.2 %copy.8 = bf16[64,7168]{1,0:T(8,128)(2,1)} copy(bf16[64,7168]{1,0:T(8,128)(2,1)} %shard_map.64) | data formatting | bytes 1835008

commit v5 on v4

--- a/solution.py
+++ b/solution.py
@@ -217,7 +217,7 @@
         near[k] = mixed(k, 0)
         return 0
 
-    lax.fori_loop(0, CHUNKS, gather, 0)
+    lax.fori_loop(0, per_core, gather, 0)
 
     def combine(i, _):
         k = chunk(i)
@@ -228,7 +228,12 @@
         arrived(far_out.at[k], far_send.at[k])
         return 0
 
-    lax.fori_loop(0, CHUNKS, combine, 0)
+    def overlap(i, _):
+        gather(i, 0)
+        return combine(i - per_core, 0)
+
+    lax.fori_loop(per_core, CHUNKS, overlap, 0)
+    lax.fori_loop(per_core, CHUNKS, combine, 0)
 
     def drain_pairs(j, _):
         mine = 2 * j + core

time: 121 us -> 121 us (level)
  no operation moved by 1% of the time
where the time goes in v5:
time: 121 us
  Pallas kernels  119 us (98%)
  local copies, waits for them, and re-layouts  2.16 us (2%)
    pallas_call x1, Pallas kernels, shards(): pl.pallas_call(functools.partial(layer_kernel, n_ep, cap), out_shape=jax....  119 us

profile of v5, /device:TPU:13, one launch (start us, length us, event | category | flops | bytes accessed | tf_op | source)
XLA Modules:
  0.0 120.9 jit_solution(15251575025546280235)
XLA Ops:
  0.0 118.7 %shard_map.64 = bf16[64,7168]{1,0:T(8,128)(2,1)} custom-call(s32[2,64]{1,0:T(2,128)} %bitcast.2, f32[2,64]{1,0:T(2,128)} %bitcast.3, bf16[64,7168]{1,0:T(8,128)(2,1)} %tok_ref.1, bf16[1,7168,512]{2,1,0:T(8,128)(2,1)} %wg_hbm.1, bf16[1,7168,512]{2,1,0:T(8,128)(2,1)} %wu_hbm.1, bf16[1,512,7168]{2,1,0:T(8,128)(2,1)} %wd_hbm.1), custom_call_target="tpu_custom_call" | custom-call | flops 8455716864 | bytes 22020096 | tf_op jit(solution)/shard_map/pallas_call | solution.py:266
  118.7 2.2 %copy.8 = bf16[64,7168]{1,0:T(8,128)(2,1)} copy(bf16[64,7168]{1,0:T(8,128)(2,1)} %shard_map.64) | data formatting | bytes 1835008
